TPU v7x, 512 devices: a whole 4x8x8 slice. The times are simulated.
512 devices in a mesh: sec: 32 (over x, y), term: 16 (over z, core).
Axes of the slice: x: 4, y: 8, z: 8, core: 2. Of those that a mesh axis runs over, the one named last changes fastest.
Arguments:
- vectors: bfloat16 [2, 32, 4, 256, 256], P(None, 'sec'), may hold values from -6 to 6
- left_ops: bfloat16 [48, 32, 256, 256], P('term', 'sec'), may hold values from -0.375 to 0.375
- right_ops: bfloat16 [48, 32, 256, 256], P('term', 'sec'), may hold values from -0.0546875 to 0.0546875
- offsets: int32 [48, 4], P('term'), may hold values from 0 to 31, as said below
Outputs:
- products: bfloat16 [2, 32, 4, 256, 256], P(None, 'sec', None, 'term')
- rayleigh: float32 [2, 2], replicated
Inputs may be any that keep to these rules, and one draw needn't show every extreme that they name: Each term's 4 offsets are distinct, and every shift from 0 to 31 occurs for some term and pair.
All inputs are finite; a program needn't handle non-finite values.
Results may differ from a plain program's by a relative error of at most 0.015.
Values may be sent and summed in bfloat16 or wider, within the bound.
A program may use at most 64 MiB of HBM per device.

v0:
```python
import jax
import jax.numpy as jnp
from jax import lax
from jax.sharding import PartitionSpec as P


def pick_blocks(carried, piece, needed):
    piece_width = piece.shape[1]
    chosen_list = []
    for pair_index in range(needed.shape[1]):
        offset_in = needed[:, pair_index]
        inside = (offset_in >= 0) & (offset_in < piece_width)
        clipped = jnp.clip(offset_in, 0, piece_width - 1)
        candidate = jnp.take_along_axis(piece, clipped[:, None, None, None], axis=1)[:, 0]
        chosen_list.append(jnp.where(inside[:, None, None], candidate, carried[pair_index]))
    return jnp.stack(chosen_list)


def local(vectors, left_ops, right_ops, offsets):
    sectors = lax.axis_size("sec")
    my_sector = lax.axis_index("sec")
    needed = (my_sector + offsets) % sectors
    local_vectors = vectors[:, 0]
    inner_part = jnp.einsum(
        "tab,ipbc->tipac", left_ops[:, 0], local_vectors, preferred_element_type=jnp.float32
    ).astype(jnp.bfloat16)
    pair_count = offsets.shape[1]
    own_right = right_ops[:, 0]
    empty_blocks = jnp.zeros((pair_count,) + own_right.shape, jnp.bfloat16)
    picked = pick_blocks(empty_blocks, lax.all_gather(right_ops, "sec", axis=1, tiled=True), needed)
    partial_value = jnp.einsum(
        "tipac,ptcd->ipad", inner_part, picked, preferred_element_type=jnp.float32
    )
    rows_share = local_vectors.shape[2] // lax.axis_size("term")
    row_start = lax.axis_index("term") * rows_share
    vector_share = lax.dynamic_slice_in_dim(local_vectors, row_start, rows_share, 2).astype(
        jnp.float32
    )
    square_part = jnp.sum(vector_share * vector_share, axis=(1, 2, 3))
    shares = lax.psum_scatter(partial_value, "term", scatter_dimension=2, tiled=True)
    gram_part = jnp.einsum("ipab,jpab->ij", vector_share, shares)
    gram_matrix, squares = lax.psum((gram_part, square_part), ("sec", "term"))
    rayleigh = gram_matrix / jnp.sqrt(squares[:, None] * squares[None, :])
    return (shares.astype(jnp.bfloat16)[:, None], rayleigh)


def solution(mesh):
    in_specs = (
        P(None, "sec", None, None, None),
        P("term", "sec", None, None),
        P("term", "sec", None, None),
        P("term", None),
    )
    out_specs = (P(None, "sec", None, "term", None), P())
    return jax.shard_map(local, mesh=mesh, in_specs=in_specs, out_specs=out_specs, check_vma=False)
```

profile of v0, /device:TPU:1, one launch (start us, length us, event | category | flops | bytes accessed | tf_op | source)
XLA Modules:
  0.0 334.2 jit_solution(14229687823892872018)
XLA Ops:
  7.2 0.7 all-gather.2.cloned.1.call-update
  7.9 1.3 dynamic-slice.1
  9.8 0.7 add_select_fusion
  10.5 0.2 clamp_reduce_fusion.3
  10.8 0.2 and_reduce_fusion.3
  11.1 0.3 multiply_reduce_fusion
  11.4 129.7 %all-gather.2.cloned.1.call-done = bf16[3,32,256,256]{3,2,1,0:T(8,128)(2,1)} async-done(((bf16[3,1,256,256]{3,2,1,0:T(8,128)(2,1)}), bf16[3,32,256,256]{3,2,1,0:T(8,128)(2,1)}) %all-gather.2.cloned.1.call-update) | async-done | bytes 12582928 | tf_op jit(solution)/shard_map/all_gather | solution.py:30
  141.1 5.2 %gather_fusion.3 = bf16[3,256,256]{2,1,0:T(8,128)(2,1)S(1)} fusion(bf16[3,32,256,256]{3,2,1,0:T(8,128)(2,1)} %all-gather.2.cloned.1.call-done, s32[3]{0:T(128)S(1)} %or_bitcast_fusion), kind=kCustom, calls=%fused_computation.3.clone | custom fusion | bytes 786456 | tf_op jit(solution)/shard_map/jit(take_along_axis)/gather | solution.py:14
  146.2 0.2 copy.19
  146.4 5.2 %gather_fusion.2 = bf16[3,256,256]{2,1,0:T(8,128)(2,1)S(1)} fusion(bf16[3,32,256,256]{3,2,1,0:T(8,128)(2,1)} %all-gather.2.cloned.1.call-done, s32[3]{0:T(128)S(1)} %or_bitcast_fusion.1), kind=kCustom, calls=%fused_computation.2.clone | custom fusion | bytes 786456 | tf_op jit(solution)/shard_map/jit(take_along_axis)/gather | solution.py:14
  151.6 0.2 copy.18
  151.7 5.2 %gather_fusion.1 = bf16[3,256,256]{2,1,0:T(8,128)(2,1)S(1)} fusion(bf16[3,32,256,256]{3,2,1,0:T(8,128)(2,1)} %all-gather.2.cloned.1.call-done, s32[3]{0:T(128)S(1)} %or_bitcast_fusion.2), kind=kCustom, calls=%fused_computation.1.clone | custom fusion | bytes 786456 | tf_op jit(solution)/shard_map/jit(take_along_axis)/gather | solution.py:14
  157.0 0.2 copy.17
  157.1 5.2 %gather_fusion = bf16[3,256,256]{2,1,0:T(8,128)(2,1)S(1)} fusion(bf16[3,32,256,256]{3,2,1,0:T(8,128)(2,1)} %all-gather.2.cloned.1.call-done, s32[3]{0:T(128)S(1)} %or_bitcast_fusion.3), kind=kCustom, calls=%fused_computation.clone | custom fusion | bytes 786456 | tf_op jit(solution)/shard_map/jit(take_along_axis)/gather | solution.py:14
  162.3 0.2 copy.16
  162.9 3.2 fusion.5
  166.2 2.2 copy.22
  168.4 59.1 %all-reduce.3 = bf16[2,4,256,256]{3,1,0,2:T(4,128)(2,1)} all-reduce(f32[2,4,256,256]{3,1,0,2:T(4,128)S(1)} %copy.22), channel_id=2, replica_groups=mesh['sec'=32,'term'=16] {'term'}, use_global_device_ids=true, to_apply=%region_0.2.clone | all-reduce | flops 524288 | bytes 3145728
  227.6 0.9 fusion.29
  228.5 0.9 constant_dynamic-slice_fusion
  229.3 0.3 convolution_bitcast_fusion
  229.6 0.7 copy.25
  230.3 96.4 %all-reduce.1 = (f32[2,2]{1,0:T(2,128)S(1)}, f32[2]{0:T(128)S(1)}) all-reduce(f32[2,2]{1,0:T(2,128)S(1)} %convolution_bitcast_fusion, f32[2]{0:T(128)S(1)} %multiply_reduce_fusion), channel_id=1, replica_groups=mesh['sec'=32,'term'=16] {'sec','term'}, use_global_device_ids=true, to_apply=%region_1.3 | all-reduce | flops 6 | bytes 48 | tf_op jit(solution)/shard_map/psum | solution.py:42
  326.7 0.6 rsqrt_multiply_fusion
  (20 shorter events, 0.6 us)
Async XLA Ops:
  7.2 3.9 %copy-start = (bf16[2,1,4,256,256]{4,3,2,1,0:T(8,128)(2,1)S(1)}, bf16[2,1,4,256,256]{4,3,2,1,0:T(8,128)(2,1)}, u32[]{:S(2)}) copy-start(bf16[2,1,4,256,256]{4,3,2,1,0:T(8,128)(2,1)} %param.6) | copy-start | bytes 3145732
  7.2 133.9 %all-gather.2.cloned.1.call-start = ((), (), s32[]{:S(2)}) async-start(), calls=%async_computation | async-start | bytes 12976128 | tf_op jit(solution)/shard_map/all_gather | solution.py:30
  151.7 11.2 %copy-start.1 = (bf16[3,1,256,256]{3,2,1,0:T(8,128)(2,1)S(1)}, bf16[3,1,256,256]{3,2,1,0:T(8,128)(2,1)}, u32[]{:S(2)}) copy-start(bf16[3,1,256,256]{3,2,1,0:T(8,128)(2,1)} %param.7) | copy-start | bytes 1179652
Sparse Core Ops, SparseCore 0:
  11.2 129.8 all-gather.1
where the time goes:
time: 335 us; the launch traced here: 334 us
  blocking collectives  156 us (47%)
  waiting for transfers between devices  130 us (39%)
  local copies, waits for them, and re-layouts  27.3 us (8%)
  between operations  14.9 us (4%)
  matrix products  3.56 us (1%)
    all_gather x1, waiting for transfers between devices, local(): lax.all_gather(right_ops, 'sec', axis=1, tiled=True)  130 us
    psum x1, blocking collectives, local(): gram_matrix, squares = lax.psum((gram_part, square_part), ('sec', 'term'))  96.4 us
    unnamed x1, blocking collectives  59.1 us
    gather x8, local copies, waits for them, and re-layouts, pick_blocks(): jnp.take_along_axis(piece, clipped[:, None, None, None], axis=1)[:, 0]  21.3 us
  transfers between devices with their start and end apart: 1, of which 1 were waited for; matrix products, arithmetic and copies ran while one was open for 1% of the time, Pallas kernels for 0%

commit v1 on v0

--- a/solution.py
+++ b/solution.py
@@ -1,7 +1,23 @@
+import functools
 import jax
 import jax.numpy as jnp
 from jax import lax
 from jax.sharding import PartitionSpec as P
+
+
+def obtain_masks(v0, group_axis, dim_at):
+    return jnp.concatenate(
+        lax.all_to_all(
+            jnp.stack([v0 for _ in range(lax.axis_size(group_axis))], axis=0),
+            group_axis,
+            split_axis=0,
+            concat_axis=0,
+        ),
+        axis=dim_at,
+    )
+
+
+lift_pages = functools.partial(obtain_masks, group_axis="sec", dim_at=1)
 
 
 def pick_blocks(carried, piece, needed):
@@ -27,7 +43,7 @@
     pair_count = offsets.shape[1]
     own_right = right_ops[:, 0]
     empty_blocks = jnp.zeros((pair_count,) + own_right.shape, jnp.bfloat16)
-    picked = pick_blocks(empty_blocks, lax.all_gather(right_ops, "sec", axis=1, tiled=True), needed)
+    picked = pick_blocks(empty_blocks, lift_pages(right_ops), needed)
     partial_value = jnp.einsum(
         "tipac,ptcd->ipad", inner_part, picked, preferred_element_type=jnp.float32
     )

time: 335 us -> 528 us (1.58)
  waiting for transfers between devices: 130 us -> 282 us
  blocking collectives: 156 us -> 182 us
  local copies, waits for them, and re-layouts: 27.3 us -> 44.9 us
  between operations: 14.9 us -> 1.49 us
  starting transfers between devices: 0.04 us -> 10.7 us
    all_to_all x0 -> x1, waiting for transfers between devices: none -> 282 us  [obtain_masks(): lax.all_to_all(jnp.stack([v0 for _ in range(lax.axis_size(group_axis))],...]
    all_gather x1 -> x0, waiting for transfers between devices: 130 us -> none  [local(): lax.all_gather(right_ops, 'sec', axis=1, tiled=True)]
    psum x1, blocking collectives: 96.4 us -> 121 us  [local(): gram_matrix, squares = lax.psum((gram_part, square_part), ('sec', 'term'))]
    all_to_all x0 -> x1, starting transfers between devices: none -> 10.7 us  [obtain_masks(): lax.all_to_all(jnp.stack([v0 for _ in range(lax.axis_size(group_axis))],...]
    all_to_all x0 -> x1, local copies, waits for them, and re-layouts: none -> 10.5 us  [obtain_masks(): lax.all_to_all(jnp.stack([v0 for _ in range(lax.axis_size(group_axis))],...]
    another operation x0 -> x1, local copies, waits for them, and re-layouts: none -> 7.11 us  [obtain_masks(): jnp.stack([v0 for _ in range(lax.axis_size(group_axis))], axis=0)]
  transfers between devices with their start and end apart: 1 -> 1, of which waited for: 1 -> 1; matrix products, arithmetic and copies ran while one was open for 1% -> 0% of each run, Pallas kernels for 0% -> 0%
where the time goes in v1:
time: 528 us
  waiting for transfers between devices  282 us (53%)
  blocking collectives  182 us (34%)
  local copies, waits for them, and re-layouts  44.9 us (9%)
  starting transfers between devices  10.7 us (2%)
    all_to_all x1, waiting for transfers between devices, obtain_masks(): lax.all_to_all(jnp.stack([v0 for _ in range(lax.axis_size(group_axis))],...  282 us
    psum x1, blocking collectives, local(): gram_matrix, squares = lax.psum((gram_part, square_part), ('sec', 'term'))  121 us
    unnamed x1, blocking collectives  60.6 us
    gather x8, local copies, waits for them, and re-layouts, pick_blocks(): jnp.take_along_axis(piece, clipped[:, None, None, None], axis=1)[:, 0]  21.3 us
    all_to_all x1, starting transfers between devices, obtain_masks(): lax.all_to_all(jnp.stack([v0 for _ in range(lax.axis_size(group_axis))],...  10.7 us
  transfers between devices with their start and end apart: 1, of which 1 were waited for; matrix products, arithmetic and copies ran while one was open for 0% of the time, Pallas kernels for 0%

profile of v1, /device:TPU:1, one launch (start us, length us, event | category | flops | bytes accessed | tf_op | source)
XLA Modules:
  0.0 527.6 jit_solution(3318012835913415932)
XLA Ops:
  0.6 7.1 %stack.4 = bf16[32,3,1,256,256]{4,3,1,2,0:T(8,128)(2,1)} broadcast(bf16[3,256,256]{2,1,0:T(8,128)(2,1)} %bitcast.132), dimensions={1,3,4} | broadcast | bytes 12976128 | tf_op jit(solution)/shard_map/stack | solution.py:11
  7.8 10.7 %all-to-all-start = ((bf16[32,3,1,256,256]{4,3,1,2,0:T(8,128)(2,1)}), bf16[32,3,1,256,256]{4,3,1,2,0:T(8,128)(2,1)}, u32[]{:S(2)}, u32[]{:S(2)}) async-start(bf16[32,3,1,256,256]{4,3,1,2,0:T(8,128)(2,1)} %stack.4), calls=%async_computation | async-start | bytes 25165824 | tf_op jit(solution)/shard_map/all_to_all | solution.py:10
  18.5 1.3 dynamic-slice.1
  20.5 0.2 clamp_reduce_fusion.3
  20.7 0.2 and_reduce_fusion.3
  21.0 0.3 multiply_reduce_fusion
  21.3 282.2 %all-to-all-done = bf16[32,3,1,256,256]{4,3,1,2,0:T(8,128)(2,1)} async-done(((bf16[32,3,1,256,256]{4,3,1,2,0:T(8,128)(2,1)}), bf16[32,3,1,256,256]{4,3,1,2,0:T(8,128)(2,1)}, u32[]{:S(2)}, u32[]{:S(2)}) %all-to-all-start) | async-done | bytes 12582944 | tf_op jit(solution)/shard_map/all_to_all | solution.py:10
  303.6 10.5 %copy.44 = bf16[32,3,1,256,256]{4,3,0,1,2:T(8,128)(2,1)} copy(bf16[32,3,1,256,256]{4,3,1,2,0:T(8,128)(2,1)} %all-to-all-done) | data formatting | bytes 25165824 | tf_op jit(solution)/shard_map/all_to_all | solution.py:10
  314.1 5.2 gather_fusion.3
  319.3 0.2 copy.20
  319.4 5.2 gather_fusion.2
  324.6 0.2 copy.19
  324.8 5.2 gather_fusion.1
  329.9 0.2 copy.18
  330.1 5.2 gather_fusion
  335.9 4.2 fusion.5
  340.1 2.2 copy.23
  342.4 60.6 %all-reduce.3 = bf16[2,4,256,256]{3,1,0,2:T(4,128)(2,1)} all-reduce(f32[2,4,256,256]{3,1,0,2:T(4,128)S(1)} %copy.23), channel_id=2, replica_groups=mesh['sec'=32,'term'=16] {'term'}, use_global_device_ids=true, to_apply=%region_0.2.clone | all-reduce | flops 524288 | bytes 3145728
  403.0 0.9 fusion.29
  403.8 0.9 constant_dynamic-slice_fusion
  404.7 0.3 convolution_bitcast_fusion
  405.0 0.7 copy.26
  405.7 121.3 %all-reduce.1 = (f32[2,2]{1,0:T(2,128)S(1)}, f32[2]{0:T(128)S(1)}) all-reduce(f32[2,2]{1,0:T(2,128)S(1)} %convolution_bitcast_fusion, f32[2]{0:T(128)S(1)} %multiply_reduce_fusion), channel_id=1, replica_groups=mesh['sec'=32,'term'=16] {'sec','term'}, use_global_device_ids=true, to_apply=%region_1.3 | all-reduce | flops 6 | bytes 48 | tf_op jit(solution)/shard_map/psum | solution.py:58
  526.9 0.6 rsqrt_multiply_fusion
  (21 shorter events, 0.7 us)
Async XLA Ops:
  0.6 20.3 %copy-start = (bf16[2,1,4,256,256]{4,3,2,1,0:T(8,128)(2,1)S(1)}, bf16[2,1,4,256,256]{4,3,2,1,0:T(8,128)(2,1)}, u32[]{:S(2)}) copy-start(bf16[2,1,4,256,256]{4,3,2,1,0:T(8,128)(2,1)} %param.6) | copy-start | bytes 3145732
  7.8 12.7 %copy-start.1 = (s32[3,4]{1,0:T(4,128)S(1)}, s32[3,4]{1,0:T(4,128)}, u32[]{:S(2)}) copy-start(s32[3,4]{1,0:T(4,128)} %param.9) | copy-start | bytes 148
  7.8 295.8 %all-to-all-start = ((bf16[32,3,1,256,256]{4,3,1,2,0:T(8,128)(2,1)}), bf16[32,3,1,256,256]{4,3,1,2,0:T(8,128)(2,1)}, u32[]{:S(2)}, u32[]{:S(2)}) async-start(bf16[32,3,1,256,256]{4,3,1,2,0:T(8,128)(2,1)} %stack.4), calls=%async_computation | async-start | bytes 25165824 | tf_op jit(solution)/shard_map/all_to_all | solution.py:10
